TPU v7x, 32 devices: a whole 2x2x4 slice. The times are simulated.
32 devices in a mesh: groups: 2 (over y), row: 2 (over x), col: 4 (over z), depth: 2 (over core).
Axes of the slice: x: 2, y: 2, z: 4, core: 2. Of those that a mesh axis runs over, the one named last changes fastest.
Arguments:
- inputs: bfloat16 [2048, 2304], P(('groups', 'row'), ('col', 'depth')), parts along dimension 0, may hold values from -6 to 6
- probe: bfloat16 [2048, 2304], P(('groups', 'row'), ('col', 'depth')), parts along dimension 0, may hold values from -6 to 6
- cotangent: bfloat16 [2048, 2304], P(('groups', 'row'), ('col', 'depth')), parts along dimension 0, may hold values from -6 to 6
- gate_weight: bfloat16 [2304, 9216], P('row', ('col', 'depth')), may hold values from -0.1875 to 0.1875
- up_weight: bfloat16 [2304, 9216], P('row', ('col', 'depth')), may hold values from -0.125 to 0.125
- down_weight: bfloat16 [9216, 2304], P(('col', 'depth'), 'row'), may hold values from -0.0625 to 0.0625
Outputs:
- hvp: bfloat16 [2048, 2304], P(('groups', 'row'), ('col', 'depth')), parts along dimension 0
There are 2 independent parts, one for each index of `groups`. A program takes and returns all parts, laid end to end along the dimension named above; an argument that names none is the same for every part. Nothing has to cross between parts.
All inputs are finite; a program needn't handle non-finite values.
Results may differ from a plain program's by a relative error of at most 0.014.
Values may be sent and summed in bfloat16 or wider, within the bound.
A program may use at most 128 MiB of HBM per device.

v0:
```python
import jax
import jax.numpy as jnp
from jax import lax
from jax.sharding import PartitionSpec as P


def gelu_tanh(value):
    return 0.5 * value * (1.0 + jnp.tanh(0.7978845608 * (value + 0.044715 * value * value * value)))


def gelu_slope(value):
    return jax.jvp(gelu_tanh, (value,), (jnp.ones_like(value),))[1]


def gelu_bend(value):
    return jax.jvp(gelu_slope, (value,), (jnp.ones_like(value),))[1]


def per_device(inputs, probe, cotangent, gate_weight, up_weight, down_weight):
    gate_full, up_full, down_full = (
        lax.all_gather(gate_weight, "row", axis=0, tiled=True),
        lax.all_gather(up_weight, "row", axis=0, tiled=True),
        lax.all_gather(down_weight, "row", axis=1, tiled=True),
    )
    in_piece = lax.all_gather(inputs, ("col", "depth"), axis=1, tiled=True)
    probe_piece = lax.all_gather(probe, ("col", "depth"), axis=1, tiled=True)
    cot_piece = lax.all_gather(cotangent, ("col", "depth"), axis=1, tiled=True)
    pre_gate = jnp.dot(in_piece, gate_full, preferred_element_type=jnp.float32)
    pre_up = jnp.dot(in_piece, up_full, preferred_element_type=jnp.float32)
    tan_gate = jnp.dot(probe_piece, gate_full, preferred_element_type=jnp.float32)
    tan_up = jnp.dot(probe_piece, up_full, preferred_element_type=jnp.float32)
    back = lax.dot_general(
        cot_piece, down_full, (((1,), (1,)), ((), ())), preferred_element_type=jnp.float32
    )
    carry = (pre_gate, pre_up, tan_gate, tan_up, back)
    pre_gate, pre_up, tan_gate, tan_up, back = carry
    slope = gelu_slope(pre_gate)
    gate_part = (back * (tan_up * slope + pre_up * gelu_bend(pre_gate) * tan_gate)).astype(
        jnp.bfloat16
    )
    up_part = (back * slope * tan_gate).astype(jnp.bfloat16)
    term = lax.dot_general(
        gate_part, gate_full, (((1,), (1,)), ((), ())), preferred_element_type=jnp.float32
    )
    term = term + lax.dot_general(
        up_part, up_full, (((1,), (1,)), ((), ())), preferred_element_type=jnp.float32
    )
    summed = lax.psum_scatter(
        term.astype(jnp.bfloat16), ("col", "depth"), scatter_dimension=1, tiled=True
    )
    return summed


def solution(mesh):
    in_specs = (
        P(("groups", "row"), ("col", "depth")),
        P(("groups", "row"), ("col", "depth")),
        P(("groups", "row"), ("col", "depth")),
        P("row", ("col", "depth")),
        P("row", ("col", "depth")),
        P(("col", "depth"), "row"),
    )
    out_specs = P(("groups", "row"), ("col", "depth"))
    return jax.shard_map(
        per_device, mesh=mesh, in_specs=in_specs, out_specs=out_specs, check_vma=False
    )
```

profile of v0, /device:TPU:0, one launch (start us, length us, event | category | flops | bytes accessed | tf_op | source)
XLA Modules:
  0.0 399.7 jit_solution(6426208478644142062)
XLA Ops:
  6.5 0.0 all-gather.15.cloned.1.call-start
  6.5 0.7 all-gather.15.cloned.1.call-update
  7.3 0.0 all-gather.17.cloned.1.call-start
  7.3 0.7 all-gather.17.cloned.1.call-update
  8.0 0.0 all-gather.11.cloned.1.call-start
  8.1 0.7 all-gather.11.cloned.1.call-update
  8.7 0.0 all-gather.7.cloned.1.call-start
  8.8 0.5 all-gather.7.cloned.1.call-update
  9.3 0.0 all-gather.9.cloned.1.call-start
  9.4 0.5 all-gather.9.cloned.1.call-update
  9.9 0.0 all-gather.13.cloned.1.call-start
  9.9 0.5 all-gather.13.cloned.1.call-update
  10.5 0.0 reduce-scatter.2.cloned.1.call-start
  10.5 32.8 %all-gather.15.cloned.1.call-done = bf16[512,2304]{0,1:T(8,128)(2,1)} async-done(((bf16[512,288]{0,1:T(8,128)(2,1)}), bf16[512,2304]{0,1:T(8,128)(2,1)}) %all-gather.15.cloned.1.call-update) | async-done | bytes 2359312 | tf_op jit(solution)/shard_map/all_gather | solution.py:25
  43.4 70.0 %all-gather.17.cloned.1.call-done = bf16[2304,1152]{1,0:T(8,128)(2,1)} async-done(((bf16[1152,1152]{1,0:T(8,128)(2,1)}), bf16[2304,1152]{1,0:T(8,128)(2,1)}) %all-gather.17.cloned.1.call-update) | async-done | bytes 5308432 | tf_op jit(solution)/shard_map/all_gather | solution.py:21
  113.3 8.0 %fusion.20 = f32[512,1152]{1,0:T(8,128)} fusion(bf16[512,2304]{0,1:T(8,128)(2,1)} %all-gather.15.cloned.1.call-done, bf16[2304,1152]{1,0:T(8,128)(2,1)} %all-gather.17.cloned.1.call-done), kind=kOutput, calls=%fused_computation.29 | convolution fusion | flops 2717908992 | bytes 10027008 | tf_op jit(solution)/shard_map/dot_general | solution.py:28
  121.3 25.4 %all-gather.11.cloned.1.call-done = bf16[512,2304]{0,1:T(8,128)(2,1)} async-done(((bf16[512,288]{0,1:T(8,128)(2,1)}), bf16[512,2304]{0,1:T(8,128)(2,1)}) %all-gather.11.cloned.1.call-update) | async-done | bytes 2359312 | tf_op jit(solution)/shard_map/all_gather | solution.py:26
  146.6 7.9 %fusion.21 = f32[512,1152]{1,0:T(8,128)} fusion(bf16[512,2304]{0,1:T(8,128)(2,1)} %all-gather.11.cloned.1.call-done, bf16[2304,1152]{1,0:T(8,128)(2,1)} %all-gather.17.cloned.1.call-done), kind=kOutput, calls=%fused_computation.30 | convolution fusion | flops 2717908992 | bytes 10027008 | tf_op jit(solution)/shard_map/dot_general | solution.py:30
  154.6 0.0 copy-start
  154.6 24.3 %all-gather.7.cloned.1.call-done = bf16[512,2304]{0,1:T(8,128)(2,1)} async-done(((bf16[512,288]{0,1:T(8,128)(2,1)}), bf16[512,2304]{0,1:T(8,128)(2,1)}) %all-gather.7.cloned.1.call-update) | async-done | bytes 2359312 | tf_op jit(solution)/shard_map/all_gather | solution.py:27
  178.9 69.8 %all-gather.9.cloned.1.call-done = bf16[1152,2304]{1,0:T(8,128)(2,1)} async-done(((bf16[1152,1152]{1,0:T(8,128)(2,1)}), bf16[1152,2304]{1,0:T(8,128)(2,1)}) %all-gather.9.cloned.1.call-update) | async-done | bytes 5308432 | tf_op jit(solution)/shard_map/all_gather | solution.py:23
  248.7 7.9 %fusion.19 = f32[512,1152]{1,0:T(8,128)} fusion(bf16[512,2304]{0,1:T(8,128)(2,1)} %all-gather.7.cloned.1.call-done, bf16[1152,2304]{1,0:T(8,128)(2,1)} %all-gather.9.cloned.1.call-done), kind=kOutput, calls=%fused_computation.28 | convolution fusion | flops 2717908992 | bytes 10027008 | tf_op jit(solution)/shard_map/dot_general | solution.py:32
  256.6 62.8 %all-gather.13.cloned.1.call-done = bf16[2304,1152]{1,0:T(8,128)(2,1)} async-done(((bf16[1152,1152]{1,0:T(8,128)(2,1)}), bf16[2304,1152]{1,0:T(8,128)(2,1)}) %all-gather.13.cloned.1.call-update) | async-done | bytes 5308432 | tf_op jit(solution)/shard_map/all_gather | solution.py:22
  319.5 0.0 copy-done
  319.5 9.7 %fusion.1 = f32[512,1152]{1,0:T(8,128)} fusion(f32[512,1152]{1,0:T(8,128)} %fusion.21, bf16[512,2304]{0,1:T(8,128)(2,1)S(1)} %copy-done, bf16[2304,1152]{1,0:T(8,128)(2,1)} %all-gather.13.cloned.1.call-done, f32[512,1152]{1,0:T(8,128)} %fusion.20), kind=kOutput, calls=%fused_computation.6 | convolution fusion | flops 2735603712 | bytes 14745600 | tf_op jit(solution)/shard_map/dot_general | solution.py:29
  329.1 0.0 copy-start.1
  329.1 17.1 %fusion.16 = f32[512,2304]{0,1:T(8,128)} fusion(bf16[2304,1152]{1,0:T(8,128)(2,1)} %all-gather.17.cloned.1.call-done, f32[512,1152]{1,0:T(8,128)} %fusion.19, f32[512,1152]{1,0:T(8,128)} %fusion.1, bf16[512,2304]{0,1:T(8,128)(2,1)} %all-gather.11.cloned.1.call-done, bf16[2304,1152]{1,0:T(8,128)(2,1)} %all-gather.13.cloned.1.call-done, f32[512,1152]{1,0:T(8,128)} %fusion.20), kind=kOutput, calls=%fused_computation.27 | convolution fusion | flops 5448794112 | bytes 24772608 | tf_op jit(solution)/shard_map/dot_general | solution.py:42
  346.2 0.0 copy-done.1
  346.2 10.3 %fusion = bf16[512,2304]{0,1:T(8,128)(2,1)} fusion(f32[512,2304]{0,1:T(8,128)} %fusion.16, bf16[2304,1152]{1,0:T(8,128)(2,1)} %all-gather.13.cloned.1.call-done, f32[512,1152]{1,0:T(8,128)} %fusion.21, f32[512,1152]{1,0:T(8,128)} %fusion.19, f32[512,1152]{1,0:T(8,128)S(1)} %copy-done.1), kind=kOutput, calls=%fused_computation.1 | convolution fusion | flops 2732654592 | bytes 19464192 | tf_op jit(solution)/shard_map/dot_general | solution.py:45
  356.5 0.0 reduce-scatter.2.cloned.1.call-update
  356.5 36.4 %reduce-scatter.2.cloned.1.call-done = bf16[512,288]{0,1:T(8,128)(2,1)} async-done(((bf16[512,2304]{0,1:T(8,128)(2,1)}), bf16[512,288]{0,1:T(8,128)(2,1)}) %reduce-scatter.2.cloned.1.call-update) | async-done | bytes 294928 | tf_op jit(solution)/shard_map/reduce_scatter | solution.py:48
Async XLA Ops:
  6.5 36.8 %all-gather.15.cloned.1.call-start = ((), (), s32[]{:S(2)}) async-start(), calls=%async_computation.5 | async-start | bytes 2654208 | tf_op jit(solution)/shard_map/all_gather | solution.py:25
  7.3 106.1 %all-gather.17.cloned.1.call-start = ((), (), s32[]{:S(2)}) async-start(), calls=%async_computation.6 | async-start | bytes 7962624 | tf_op jit(solution)/shard_map/all_gather | solution.py:21
  8.0 138.6 %all-gather.11.cloned.1.call-start = ((), (), s32[]{:S(2)}) async-start(), calls=%async_computation.3 | async-start | bytes 2654208 | tf_op jit(solution)/shard_map/all_gather | solution.py:26
  8.7 170.2 %all-gather.7.cloned.1.call-start = ((), (), s32[]{:S(2)}) async-start(), calls=%async_computation.1 | async-start | bytes 2654208 | tf_op jit(solution)/shard_map/all_gather | solution.py:27
  9.3 239.4 %all-gather.9.cloned.1.call-start = ((), (), s32[]{:S(2)}) async-start(), calls=%async_computation.2 | async-start | bytes 7962624 | tf_op jit(solution)/shard_map/all_gather | solution.py:23
  9.9 309.6 %all-gather.13.cloned.1.call-start = ((), (), s32[]{:S(2)}) async-start(), calls=%async_computation.4 | async-start | bytes 7962624 | tf_op jit(solution)/shard_map/all_gather | solution.py:22
  10.5 382.4 %reduce-scatter.2.cloned.1.call-start = ((), (), s32[]{:S(2)}) async-start(), calls=%async_computation.7 | async-start | bytes 2654208 | tf_op jit(solution)/shard_map/reduce_scatter | solution.py:48
  154.6 164.9 %copy-start = (bf16[512,2304]{0,1:T(8,128)(2,1)S(1)}, bf16[512,2304]{0,1:T(8,128)(2,1)}, u32[]{:S(2)}) copy-start(bf16[512,2304]{0,1:T(8,128)(2,1)} %all-gather.15.cloned.1.call-done) | copy-start | bytes 7077892
  329.1 17.1 %copy-start.1 = (f32[512,1152]{1,0:T(8,128)S(1)}, f32[512,1152]{1,0:T(8,128)}, u32[]{:S(2)}) copy-start(f32[512,1152]{1,0:T(8,128)} %fusion.20) | copy-start | bytes 7077892
Sparse Core Ops, SparseCore 0:
  9.0 34.3 all-gather.14
  44.9 68.3 all-gather.16
  115.0 31.6 all-gather.10
  148.1 30.7 all-gather.6
  180.3 68.3 all-gather.8
  250.1 69.2 all-gather.12
  356.6 36.2 reduce-scatter.1
where the time goes:
time: 400 us
  waiting for transfers between devices  325 us (81%)
  matrix products  60.8 us (15%)
  between operations  13.5 us (3%)
    all_gather x1, waiting for transfers between devices, per_device(): lax.all_gather(gate_weight, 'row', axis=0, tiled=True)  70 us
    all_gather x1, waiting for transfers between devices, per_device(): lax.all_gather(down_weight, 'row', axis=1, tiled=True)  69.8 us
    all_gather x1, waiting for transfers between devices, per_device(): lax.all_gather(up_weight, 'row', axis=0, tiled=True)  62.8 us
    reduce_scatter x1, waiting for transfers between devices, per_device(): lax.psum_scatter(term.astype(jnp.bfloat16), ('col', 'depth'), scatter_dim...  36.4 us
    all_gather x1, waiting for transfers between devices, per_device(): in_piece = lax.all_gather(inputs, ('col', 'depth'), axis=1, tiled=True)  32.8 us
    all_gather x1, waiting for transfers between devices, per_device(): probe_piece = lax.all_gather(probe, ('col', 'depth'), axis=1, tiled=True)  25.4 us
    all_gather x1, waiting for transfers between devices, per_device(): cot_piece = lax.all_gather(cotangent, ('col', 'depth'), axis=1, tiled=True)  24.3 us
    dot_general x1, matrix products, per_device(): lax.dot_general(gate_part, gate_full, (((1,), (1,)), ((), ())), preferred...  17.1 us
  transfers between devices with their start and end apart: 7, of which 7 were waited for; matrix products, arithmetic and copies ran while one was open for 6% of the time, Pallas kernels for 0%

commit v1 on v0

v1 whole, which is shorter than its diff:
```python
import functools

import jax
import jax.numpy as jnp
from jax import lax
from jax.experimental import pallas as pl
from jax.experimental.pallas import tpu as pltpu
from jax.sharding import PartitionSpec as P

MESH = pl.DeviceIdType.MESH
F32, BF16 = jnp.float32, jnp.bfloat16
K0, K1 = 0.7978845608, 0.044715
PIECE = 128
WIDE = 256


def gelu_tanh(value):
    return 0.5 * value * (1.0 + jnp.tanh(K0 * (value + K1 * value * value * value)))


def gelu_slope(value):
    return jax.jvp(gelu_tanh, (value,), (jnp.ones_like(value),))[1]


def gelu_bend(value):
    return jax.jvp(gelu_slope, (value,), (jnp.ones_like(value),))[1]


def slope_and_bend(s):
    sq = s * s
    t = jnp.tanh(K0 * s * (1.0 + K1 * sq))
    du = K0 + (3.0 * K0 * K1) * sq
    e = 1.0 - t * t
    slope = 0.5 * (1.0 + t) + 0.5 * s * e * du
    bend = e * (K0 + (6.0 * K0 * K1) * sq - s * t * du * du)
    return slope, bend


def nt(a, b):
    return lax.dot_general(a, b, (((1,), (1,)), ((), ())), preferred_element_type=F32)


def nn(a, b):
    return jnp.dot(a, b, preferred_element_type=F32)


def kernel(
    n, acts_ref, gw_ref, uw_ref, dw_ref, out_ref,
    xt, xs, cot, own_g, own_u, own_d, far_g, far_u, far_d, acc,
    sib_out, sib_in, z_out, z_in,
    own_sem, xsend, xrecv, ysend, yrecv, rsend, rrecv, lsend, lrecv, ssend, srecv,
    qsend, qrecv, zsend, zrecv,
):
    g, r = lax.axis_index("groups"), lax.axis_index("row")
    c, d = lax.axis_index("col"), lax.axis_index("depth")
    half, hidden = gw_ref.shape
    part, tokens = acts_ref.shape[1:]
    pieces = hidden // PIECE
    hd = half // 2

    def at(gg=g, rr=r, cc=c, dd=d):
        return (gg, rr, cc, dd)

    x_dev, y_dev, sib = at(rr=1 - r), at(gg=1 - g), at(dd=1 - d)

    def rows_of(cc, dd):
        return pl.ds(pl.multiple_of((cc * 2 + dd) * part, 32), part)

    own_copies = [
        pltpu.make_async_copy(acts_ref, xt.at[:, rows_of(c, d), :], own_sem.at[0]),
        pltpu.make_async_copy(gw_ref, own_g, own_sem.at[1]),
        pltpu.make_async_copy(uw_ref, own_u, own_sem.at[2]),
        pltpu.make_async_copy(dw_ref, own_d, own_sem.at[3]),
    ]
    for cp in own_copies:
        cp.start()

    barrier = pltpu.get_barrier_semaphore()
    for dev in (x_dev, y_dev, sib):
        pl.semaphore_signal(barrier, inc=1, device_id=dev, device_id_type=MESH)
    for k in range(1, n):
        pl.semaphore_signal(
            barrier, inc=1, device_id=at(cc=lax.rem(c + k, n)), device_id_type=MESH
        )
    pl.semaphore_wait(barrier, n + 2)

    def windows(j, w):
        col = pl.ds(pl.multiple_of(j * PIECE, PIECE), PIECE)
        row = pl.ds(pl.multiple_of(w * hd, 32), hd)
        hrow = pl.ds(pl.multiple_of(j * PIECE + w * (PIECE // 2), 64), PIECE // 2)
        return (row, col), (row, col), (hrow, slice(None))

    def x_copy(j, a):
        win = windows(j, g)[a]
        return pltpu.make_async_remote_copy(
            src_ref=(gw_ref, uw_ref, dw_ref)[a].at[win],
            dst_ref=(far_g, far_u, far_d)[a].at[win],
            send_sem=xsend.at[j, a], recv_sem=xrecv.at[j, a],
            device_id=x_dev, device_id_type=MESH,
        )

    def y_copy(j, a, w):
        win = windows(j, w)[a]
        far = (far_g, far_u, far_d)[a].at[win]
        return pltpu.make_async_remote_copy(
            src_ref=far, dst_ref=far,
            send_sem=ysend.at[j, a], recv_sem=yrecv.at[j, a],
            device_id=y_dev, device_id_type=MESH,
        )

    def x_start(j):
        for a in range(3):
            x_copy(j, a).start()

    def forward(j):
        for a in range(3):
            x_copy(j, a).wait_recv()
            y_copy(j, a, g).start()

    def y_arrived(j):
        for a in range(3):
            y_copy(j, a, 1 - g).wait_recv()

    def z_copy(s, right):
        src = c - s if right else c + s
        blk = xt.at[:, rows_of(src, d), :]
        return pltpu.make_async_remote_copy(
            src_ref=acts_ref if s == 0 else blk, dst_ref=blk,
            send_sem=(rsend if right else lsend).at[s],
            recv_sem=(rrecv if right else lrecv).at[s],
            device_id=at(cc=c + 1 if right else c - 1), device_id_type=MESH,
        )

    def z_arrival(s, right):
        src = c - 1 - s if right else c + 1 + s
        blk = xt.at[:, rows_of(src, d), :]
        return pltpu.make_async_remote_copy(
            src_ref=blk, dst_ref=blk,
            send_sem=(rsend if right else lsend).at[s],
            recv_sem=(rrecv if right else lrecv).at[s],
            device_id=at(cc=c - 1 if right else c + 1), device_id_type=MESH,
        )

    def sib_copy(src, own=False, dd=d):
        blk = xt.at[:, rows_of(src, dd), :]
        return pltpu.make_async_remote_copy(
            src_ref=acts_ref if own else blk, dst_ref=blk,
            send_sem=ssend.at[src], recv_sem=srecv.at[src],
            device_id=sib, device_id_type=MESH,
        )

    def sends(s, right):
        return (c + 1 < n) & (c - s >= 0) if right else (c >= 1) & (c + s < n)

    def gets(s, right):
        return c - 1 - s >= 0 if right else c + 1 + s < n

    def z_start(s, right):
        @pl.when(sends(s, right))
        def _():
            z_copy(s, right).start()

    def z_got(s, right):
        @pl.when(gets(s, right))
        def _():
            z_arrival(s, right).wait_recv()

        if s + 1 < n - 1:
            z_start(s + 1, right)

        @pl.when(gets(s, right))
        def _():
            sib_copy(c - 1 - s if right else c + 1 + s).start()

    x_start(0)
    z_start(0, True)
    z_start(0, False)
    sib_copy(c, own=True).start()
    x_start(1)
    x_start(2)
    acc[...] = jnp.zeros_like(acc)

    lead = 2 * (n - 1)
    for j in range(lead):
        forward(j)
        if j + 3 < pieces:
            x_start(j + 3)
        if j % 2:
            z_got(j // 2, True)
            z_got(j // 2, False)

    for cp in own_copies:
        cp.wait()
    for src in range(n):
        sib_copy(src, dd=1 - d).wait_recv()

    blocks = half // 128
    for h in range(2):
        @pl.loop(0, blocks)
        def _(j):
            feat = pl.ds(pl.multiple_of(h * half + j * 128, 128), 128)
            lane = pl.ds(pl.multiple_of(j * 128, 128), 128)
            xs[h, :tokens, lane] = xt[0, feat, :].T
            xs[h, tokens:, lane] = xt[1, feat, :].T
            cot[h, :, lane] = xt[2, feat, :].T

    def compute(off, width):
        col = pl.ds(off, width)
        gates = nn(xs[r], own_g[:, col]) + nn(xs[1 - r], far_g[:, col])
        ups = nn(xs[r], own_u[:, col]) + nn(xs[1 - r], far_u[:, col])
        back = nt(cot[r], own_d[col, :]) + nt(cot[1 - r], far_d[col, :])
        pre_gate, tan_gate = gates[:tokens], gates[tokens:]
        pre_up, tan_up = ups[:tokens], ups[tokens:]
        slope, bend = slope_and_bend(pre_gate)
        gate_part = (back * (tan_up * slope + pre_up * bend * tan_gate)).astype(BF16)
        up_part = (back * slope * tan_gate).astype(BF16)
        for w_g, w_u, base in ((own_g, own_u, r), (far_g, far_u, 1 - r)):
            for q in range(0, half, part):
                rows = pl.ds(pl.multiple_of(base * half + q, 32), part)
                acc[rows, :] += nt(w_g[q:q + part, col], gate_part) + nt(
                    w_u[q:q + part, col], up_part
                )

    per = WIDE // PIECE
    steps = hidden // WIDE

    @pl.loop(0, steps)
    def _(i):
        for k in range(per):
            y_arrived(i * per + k)

        @pl.when(lead + i < pieces)
        def _():
            forward(lead + i)

        compute(pl.multiple_of(i * WIDE, WIDE), WIDE)

    for j in range(lead + steps, pieces):
        forward(j)
    for j in range(steps * per, pieces):
        y_arrived(j)
        compute(j * PIECE, PIECE)

    def q_copy(cc):
        return pltpu.make_async_remote_copy(
            src_ref=sib_out.at[cc], dst_ref=sib_in.at[cc],
            send_sem=qsend.at[cc], recv_sem=qrecv.at[cc],
            device_id=sib, device_id_type=MESH,
        )

    for cc in range(n):
        sib_out[cc] = acc[rows_of(cc, 1 - d), :].astype(BF16)
        q_copy(cc).start()

    def zr_copy(k):
        to = lax.rem(c + k, n)
        return pltpu.make_async_remote_copy(
            src_ref=z_out.at[k - 1], dst_ref=z_in.at[k - 1],
            send_sem=zsend.at[k - 1], recv_sem=zrecv.at[k - 1],
            device_id=at(cc=to), device_id_type=MESH,
        )

    for cc in range(n):
        q_copy(cc).wait_recv()
    for k in range(1, n):
        to = lax.rem(c + k, n)
        z_out[k - 1] = (acc[rows_of(to, d), :] + sib_in[to].astype(F32)).astype(BF16)
        zr_copy(k).start()
    total = acc[rows_of(c, d), :] + sib_in[c].astype(F32)
    for k in range(1, n):
        zr_copy(k).wait_recv()
        total = total + z_in[k - 1].astype(F32)
    out_ref[...] = total.astype(BF16)

    @pl.loop(0, pieces)
    def _(j):
        for a in range(3):
            x_copy(j, a).wait_send()
            y_copy(j, a, g).wait_send()

    for s in range(n - 1):
        for right in (True, False):
            @pl.when(sends(s, right))
            def _():
                z_copy(s, right).wait_send()
    for cc in range(n):
        sib_copy(cc).wait_send()
        q_copy(cc).wait_send()
    for k in range(1, n):
        zr_copy(k).wait_send()


def fused(n, inputs, probe, cotangent, gate_weight, up_weight, down_weight):
    tokens, part = inputs.shape
    half, hidden = gate_weight.shape
    wide = 2 * half
    pieces = hidden // PIECE
    acts = jnp.stack([inputs, probe, cotangent]).transpose(0, 2, 1)
    dma = pltpu.SemaphoreType.DMA
    any_spec = pl.BlockSpec(memory_space=pl.ANY)
    vmem = pltpu.VMEM
    out = pl.pallas_call(
        functools.partial(kernel, n),
        out_shape=jax.ShapeDtypeStruct((part, tokens), BF16),
        in_specs=[any_spec] * 4,
        out_specs=pl.BlockSpec(memory_space=pltpu.VMEM),
        scratch_shapes=[
            vmem((3, wide, tokens), BF16),
            vmem((2, 2 * tokens, half), BF16),
            vmem((2, tokens, half), BF16),
            vmem((half, hidden), BF16), vmem((half, hidden), BF16), vmem((hidden, half), BF16),
            vmem((half, hidden), BF16), vmem((half, hidden), BF16), vmem((hidden, half), BF16),
            vmem((wide, tokens), F32),
            vmem((n, part, tokens), BF16), vmem((n, part, tokens), BF16),
            vmem((n - 1, part, tokens), BF16), vmem((n - 1, part, tokens), BF16),
            dma((4,)),
            dma((pieces, 3)), dma((pieces, 3)), dma((pieces, 3)), dma((pieces, 3)),
            dma((n - 1,)), dma((n - 1,)), dma((n - 1,)), dma((n - 1,)),
            dma((n,)), dma((n,)), dma((n,)), dma((n,)),
            dma((n - 1,)), dma((n - 1,)),
        ],
        compiler_params=pltpu.CompilerParams(
            collective_id=0, has_side_effects=True, vmem_limit_bytes=60 * 2**20
        ),
        cost_estimate=pl.CostEstimate(
            flops=14 * tokens * wide * hidden,
            bytes_accessed=6 * half * hidden,
            transcendentals=tokens * hidden,
        ),
    )(acts, gate_weight, up_weight, down_weight)
    return out.T


def gathered(inputs, probe, cotangent, gate_weight, up_weight, down_weight):
    gate_full, up_full, down_full = (
        lax.all_gather(gate_weight, "row", axis=0, tiled=True),
        lax.all_gather(up_weight, "row", axis=0, tiled=True),
        lax.all_gather(down_weight, "row", axis=1, tiled=True),
    )
    in_piece = lax.all_gather(inputs, ("col", "depth"), axis=1, tiled=True)
    probe_piece = lax.all_gather(probe, ("col", "depth"), axis=1, tiled=True)
    cot_piece = lax.all_gather(cotangent, ("col", "depth"), axis=1, tiled=True)
    pre_gate, pre_up = nn(in_piece, gate_full), nn(in_piece, up_full)
    tan_gate, tan_up = nn(probe_piece, gate_full), nn(probe_piece, up_full)
    back = nt(cot_piece, down_full)
    slope = gelu_slope(pre_gate)
    gate_part = (back * (tan_up * slope + pre_up * gelu_bend(pre_gate) * tan_gate)).astype(BF16)
    up_part = (back * slope * tan_gate).astype(BF16)
    term = nt(gate_part, gate_full) + nt(up_part, up_full)
    return lax.psum_scatter(
        term.astype(BF16), ("col", "depth"), scatter_dimension=1, tiled=True
    )


def solution(mesh):
    sizes = dict(mesh.shape)
    n = sizes["col"]

    def per_device(*args):
        half, hidden = args[3].shape
        square = sizes["groups"] == 2 and sizes["row"] == 2 and sizes["depth"] == 2
        even = half % 128 == 0 and hidden % PIECE == 0 and args[0].shape[1] % 32 == 0
        small = 2 * (n - 1) <= hidden // PIECE and half * hidden <= 2**21
        if square and even and small:
            return fused(n, *args)
        return gathered(*args)

    in_specs = (
        P(("groups", "row"), ("col", "depth")),
        P(("groups", "row"), ("col", "depth")),
        P(("groups", "row"), ("col", "depth")),
        P("row", ("col", "depth")),
        P("row", ("col", "depth")),
        P(("col", "depth"), "row"),
    )
    out_specs = P(("groups", "row"), ("col", "depth"))
    return jax.shard_map(
        per_device, mesh=mesh, in_specs=in_specs, out_specs=out_specs, check_vma=False
    )
```

time: 400 us -> 143 us (0.36)
  the two profiles are of different devices: /device:TPU:0 before, /device:TPU:9 now
where the time goes in v1:
time: 143 us
  Pallas kernels  139 us (97%)
  other arithmetic  2.16 us (2%)
  local copies, waits for them, and re-layouts  1.69 us (1%)
    pallas_call x1, Pallas kernels, fused(): pl.pallas_call(functools.partial(kernel, n), out_shape=jax.ShapeDtypeStru...  139 us

profile of v1, /device:TPU:9, one launch (start us, length us, event | category | flops | bytes accessed | tf_op | source)
XLA Modules:
  0.0 142.8 jit_solution(9034308606652866343)
XLA Ops:
  0.0 2.2 %maximum_bitcast_fusion.acts_ref = bf16[3,288,512]{2,1,0:T(8,128)(2,1)} fusion(bf16[1,512,288]{1,2,0:T(8,128)(2,1)} %bitcast.6, bf16[1,512,288]{1,2,0:T(8,128)(2,1)} %bitcast.7, bf16[1,512,288]{1,2,0:T(8,128)(2,1)} %bitcast.8), kind=kLoop, calls=%fused_computation | loop fusion | flops 884736 | bytes 1769472 | tf_op jit(solution)/shard_map/transpose | solution.py:298
  2.2 139.0 %shard_map.64 = bf16[288,512]{1,0:T(8,128)(2,1)} custom-call(bf16[3,288,512]{2,1,0:T(8,128)(2,1)} %maximum_bitcast_fusion.acts_ref, bf16[1152,1152]{1,0:T(8,128)(2,1)} %gw_ref.1, bf16[1152,1152]{1,0:T(8,128)(2,1)} %uw_ref.1, bf16[1152,1152]{1,0:T(8,128)(2,1)} %dw_ref.1), custom_call_target="tpu_custom_call" | custom-call | flops 19025362944 | bytes 7962624 | tf_op jit(solution)/shard_map/pallas_call | solution.py:302
  141.2 1.7 %copy.8 = bf16[512,288]{0,1:T(8,128)(2,1)} copy(bf16[512,288]{0,1:T(8,128)(2,1)} %bitcast.9) | data formatting | bytes 589824

commit v2 on v1

--- a/solution.py
+++ b/solution.py
@@ -45,8 +45,8 @@
 
 
 def kernel(
-    n, acts_ref, gw_ref, uw_ref, dw_ref, out_ref,
-    xt, xs, cot, own_g, own_u, own_d, far_g, far_u, far_d, acc,
+    n, in_ref, pr_ref, ct_ref, gw_ref, uw_ref, dw_ref, out_ref,
+    raw, xt, xs, cot, own_g, own_u, own_d, far_g, far_u, far_d, acc,
     sib_out, sib_in, z_out, z_in,
     own_sem, xsend, xrecv, ysend, yrecv, rsend, rrecv, lsend, lrecv, ssend, srecv,
     qsend, qrecv, zsend, zrecv,
@@ -54,7 +54,7 @@
     g, r = lax.axis_index("groups"), lax.axis_index("row")
     c, d = lax.axis_index("col"), lax.axis_index("depth")
     half, hidden = gw_ref.shape
-    part, tokens = acts_ref.shape[1:]
+    tokens, part = in_ref.shape
     pieces = hidden // PIECE
     hd = half // 2
 
@@ -67,12 +67,15 @@
         return pl.ds(pl.multiple_of((cc * 2 + dd) * part, 32), part)
 
     own_copies = [
-        pltpu.make_async_copy(acts_ref, xt.at[:, rows_of(c, d), :], own_sem.at[0]),
-        pltpu.make_async_copy(gw_ref, own_g, own_sem.at[1]),
-        pltpu.make_async_copy(uw_ref, own_u, own_sem.at[2]),
-        pltpu.make_async_copy(dw_ref, own_d, own_sem.at[3]),
+        pltpu.make_async_copy(gw_ref, own_g, own_sem.at[0]),
+        pltpu.make_async_copy(uw_ref, own_u, own_sem.at[1]),
+        pltpu.make_async_copy(dw_ref, own_d, own_sem.at[2]),
     ]
-    for cp in own_copies:
+    raw_copies = [
+        pltpu.make_async_copy(ref, raw.at[a], own_sem.at[3 + a])
+        for a, ref in enumerate((in_ref, pr_ref, ct_ref))
+    ]
+    for cp in raw_copies:
         cp.start()
 
     barrier = pltpu.get_barrier_semaphore()
@@ -125,7 +128,7 @@
         src = c - s if right else c + s
         blk = xt.at[:, rows_of(src, d), :]
         return pltpu.make_async_remote_copy(
-            src_ref=acts_ref if s == 0 else blk, dst_ref=blk,
+            src_ref=blk, dst_ref=blk,
             send_sem=(rsend if right else lsend).at[s],
             recv_sem=(rrecv if right else lrecv).at[s],
             device_id=at(cc=c + 1 if right else c - 1), device_id_type=MESH,
@@ -141,10 +144,10 @@
             device_id=at(cc=c - 1 if right else c + 1), device_id_type=MESH,
         )
 
-    def sib_copy(src, own=False, dd=d):
+    def sib_copy(src, dd=d):
         blk = xt.at[:, rows_of(src, dd), :]
         return pltpu.make_async_remote_copy(
-            src_ref=acts_ref if own else blk, dst_ref=blk,
+            src_ref=blk, dst_ref=blk,
             send_sem=ssend.at[src], recv_sem=srecv.at[src],
             device_id=sib, device_id_type=MESH,
         )
@@ -172,12 +175,16 @@
         def _():
             sib_copy(c - 1 - s if right else c + 1 + s).start()
 
-    x_start(0)
+    for j in range(3):
+        x_start(j)
+    for a in range(3):
+        raw_copies[a].wait()
+        xt[a, rows_of(c, d), :] = raw[a].T
     z_start(0, True)
     z_start(0, False)
-    sib_copy(c, own=True).start()
-    x_start(1)
-    x_start(2)
+    sib_copy(c).start()
+    for cp in own_copies:
+        cp.start()
     acc[...] = jnp.zeros_like(acc)
 
     lead = 2 * (n - 1)
@@ -229,11 +236,11 @@
         for k in range(per):
             y_arrived(i * per + k)
 
+        compute(pl.multiple_of(i * WIDE, WIDE), WIDE)
+
         @pl.when(lead + i < pieces)
         def _():
             forward(lead + i)
-
-        compute(pl.multiple_of(i * WIDE, WIDE), WIDE)
 
     for j in range(lead + steps, pieces):
         forward(j)
@@ -248,29 +255,56 @@
             device_id=sib, device_id_type=MESH,
         )
 
-    for cc in range(n):
-        sib_out[cc] = acc[rows_of(cc, 1 - d), :].astype(BF16)
-        q_copy(cc).start()
-
-    def zr_copy(k):
-        to = lax.rem(c + k, n)
-        return pltpu.make_async_remote_copy(
-            src_ref=z_out.at[k - 1], dst_ref=z_in.at[k - 1],
-            send_sem=zsend.at[k - 1], recv_sem=zrecv.at[k - 1],
-            device_id=at(cc=to), device_id_type=MESH,
-        )
-
-    for cc in range(n):
-        q_copy(cc).wait_recv()
-    for k in range(1, n):
-        to = lax.rem(c + k, n)
-        z_out[k - 1] = (acc[rows_of(to, d), :] + sib_in[to].astype(F32)).astype(BF16)
-        zr_copy(k).start()
-    total = acc[rows_of(c, d), :] + sib_in[c].astype(F32)
-    for k in range(1, n):
-        zr_copy(k).wait_recv()
-        total = total + z_in[k - 1].astype(F32)
-    out_ref[...] = total.astype(BF16)
+    side = (2 * c) // n
+
+    def q_order(i):
+        return (n - 1 - i) * (1 - side) + i * side
+
+    for i in range(n):
+        t = q_order(i)
+        sib_out[t] = acc[rows_of(t, 1 - d), :].astype(BF16)
+        q_copy(t).start()
+
+    def z_sum(way, t):
+        return pltpu.make_async_remote_copy(
+            src_ref=z_out.at[t], dst_ref=z_in.at[way, t],
+            send_sem=zsend.at[t], recv_sem=zrecv.at[way, t],
+            device_id=at(cc=c + 1 - 2 * way), device_id_type=MESH,
+        )
+
+    def z_came(way, t):
+        return pltpu.make_async_remote_copy(
+            src_ref=z_out.at[t], dst_ref=z_in.at[way, t],
+            send_sem=zsend.at[t], recv_sem=zrecv.at[way, t],
+            device_id=at(cc=c - 1 + 2 * way), device_id_type=MESH,
+        )
+
+    def fed(way):
+        return c * (1 - way) + (n - 1 - c) * way > 0
+
+    def add_in(way, t):
+        @pl.when(fed(way))
+        def _():
+            z_came(way, t).wait_recv()
+            rows = rows_of(t, d)
+            acc[rows, :] += z_in[way, t].astype(F32)
+
+    def pass_on(way, t):
+        @pl.when((t - c) * (1 - 2 * way) > 0)
+        def _():
+            add_in(way, t)
+            z_out[t] = (acc[rows_of(t, d), :] + sib_in[t].astype(F32)).astype(BF16)
+            z_sum(way, t).start()
+
+    for i in range(n):
+        t = q_order(i)
+        q_copy(t).wait_recv()
+        pass_on(side, t)
+    for i in range(n - 1):
+        pass_on(1 - side, n - 1 - q_order(i))
+    add_in(side, c)
+    add_in(1 - side, c)
+    out_ref[...] = (acc[rows_of(c, d), :] + sib_in[c].astype(F32)).astype(BF16)
 
     @pl.loop(0, pieces)
     def _(j):
@@ -286,8 +320,11 @@
     for cc in range(n):
         sib_copy(cc).wait_send()
         q_copy(cc).wait_send()
-    for k in range(1, n):
-        zr_copy(k).wait_send()
+    for t in range(n):
+        for way, away in ((0, t > c), (1, t < c)):
+            @pl.when(away)
+            def _():
+                z_sum(way, t).wait_send()
 
 
 def fused(n, inputs, probe, cotangent, gate_weight, up_weight, down_weight):
@@ -295,16 +332,16 @@
     half, hidden = gate_weight.shape
     wide = 2 * half
     pieces = hidden // PIECE
-    acts = jnp.stack([inputs, probe, cotangent]).transpose(0, 2, 1)
     dma = pltpu.SemaphoreType.DMA
     any_spec = pl.BlockSpec(memory_space=pl.ANY)
     vmem = pltpu.VMEM
     out = pl.pallas_call(
         functools.partial(kernel, n),
         out_shape=jax.ShapeDtypeStruct((part, tokens), BF16),
-        in_specs=[any_spec] * 4,
+        in_specs=[any_spec] * 6,
         out_specs=pl.BlockSpec(memory_space=pltpu.VMEM),
         scratch_shapes=[
+            vmem((3, tokens, part), BF16),
             vmem((3, wide, tokens), BF16),
             vmem((2, 2 * tokens, half), BF16),
             vmem((2, tokens, half), BF16),
@@ -312,12 +349,12 @@
             vmem((half, hidden), BF16), vmem((half, hidden), BF16), vmem((hidden, half), BF16),
             vmem((wide, tokens), F32),
             vmem((n, part, tokens), BF16), vmem((n, part, tokens), BF16),
-            vmem((n - 1, part, tokens), BF16), vmem((n - 1, part, tokens), BF16),
-            dma((4,)),
+            vmem((n, part, tokens), BF16), vmem((2, n, part, tokens), BF16),
+            dma((6,)),
             dma((pieces, 3)), dma((pieces, 3)), dma((pieces, 3)), dma((pieces, 3)),
             dma((n - 1,)), dma((n - 1,)), dma((n - 1,)), dma((n - 1,)),
             dma((n,)), dma((n,)), dma((n,)), dma((n,)),
-            dma((n - 1,)), dma((n - 1,)),
+            dma((n,)), dma((2, n)),
         ],
         compiler_params=pltpu.CompilerParams(
             collective_id=0, has_side_effects=True, vmem_limit_bytes=60 * 2**20
@@ -327,7 +364,7 @@
             bytes_accessed=6 * half * hidden,
             transcendentals=tokens * hidden,
         ),
-    )(acts, gate_weight, up_weight, down_weight)
+    )(inputs, probe, cotangent, gate_weight, up_weight, down_weight)
     return out.T
 
 

time: 143 us -> 143 us (level)
  the two profiles are of different devices: /device:TPU:9 before, /device:TPU:0 now
where the time goes in v2:
time: 143 us
  Pallas kernels  135 us (94%)
  local copies, waits for them, and re-layouts  7.32 us (5%)
    pallas_call x1, Pallas kernels, fused(): pl.pallas_call(functools.partial(kernel, n), out_shape=jax.ShapeDtypeStru...  135 us
    unnamed x4, local copies, waits for them, and re-layouts  7.32 us

profile of v2, /device:TPU:0, one launch (start us, length us, event | category | flops | bytes accessed | tf_op | source)
XLA Modules:
  0.0 142.5 jit_solution(10811214749383472555)
XLA Ops:
  0.0 1.9 %copy.7.in_ref = bf16[512,288]{1,0:T(8,128)(2,1)} copy(bf16[512,288]{0,1:T(8,128)(2,1)} %param.6) | data formatting | bytes 589824 | tf_op args[0]
  1.9 1.9 %copy.8.pr_ref = bf16[512,288]{1,0:T(8,128)(2,1)} copy(bf16[512,288]{0,1:T(8,128)(2,1)} %param.7) | data formatting | bytes 589824 | tf_op args[1]
  3.8 1.9 %copy.9.ct_ref = bf16[512,288]{1,0:T(8,128)(2,1)} copy(bf16[512,288]{0,1:T(8,128)(2,1)} %param.8) | data formatting | bytes 589824 | tf_op args[2]
  5.6 135.2 %shard_map.64 = bf16[288,512]{1,0:T(8,128)(2,1)} custom-call(bf16[512,288]{1,0:T(8,128)(2,1)} %copy.7.in_ref, bf16[512,288]{1,0:T(8,128)(2,1)} %copy.8.pr_ref, bf16[512,288]{1,0:T(8,128)(2,1)} %copy.9.ct_ref, bf16[1152,1152]{1,0:T(8,128)(2,1)} %gw_ref.1, bf16[1152,1152]{1,0:T(8,128)(2,1)} %uw_ref.1, bf16[1152,1152]{1,0:T(8,128)(2,1)} %dw_ref.1), custom_call_target="tpu_custom_call" | custom-call | flops 19025362944 | bytes 7962624 | tf_op jit(solution)/shard_map/pallas_call | solution.py:338
  140.8 1.7 %copy.11 = bf16[512,288]{0,1:T(8,128)(2,1)} copy(bf16[512,288]{0,1:T(8,128)(2,1)} %bitcast.1) | data formatting | bytes 589824

commit v3 on v2

--- a/solution.py
+++ b/solution.py
@@ -46,7 +46,7 @@
 
 def kernel(
     n, in_ref, pr_ref, ct_ref, gw_ref, uw_ref, dw_ref, out_ref,
-    raw, xt, xs, cot, own_g, own_u, own_d, far_g, far_u, far_d, acc,
+    xt, xs, cot, own_g, own_u, own_d, far_g, far_u, far_d, acc,
     sib_out, sib_in, z_out, z_in,
     own_sem, xsend, xrecv, ysend, yrecv, rsend, rrecv, lsend, lrecv, ssend, srecv,
     qsend, qrecv, zsend, zrecv,
@@ -54,7 +54,7 @@
     g, r = lax.axis_index("groups"), lax.axis_index("row")
     c, d = lax.axis_index("col"), lax.axis_index("depth")
     half, hidden = gw_ref.shape
-    tokens, part = in_ref.shape
+    part, tokens = in_ref.shape
     pieces = hidden // PIECE
     hd = half // 2
 
@@ -72,7 +72,7 @@
         pltpu.make_async_copy(dw_ref, own_d, own_sem.at[2]),
     ]
     raw_copies = [
-        pltpu.make_async_copy(ref, raw.at[a], own_sem.at[3 + a])
+        pltpu.make_async_copy(ref, xt.at[a, rows_of(c, d), :], own_sem.at[3 + a])
         for a, ref in enumerate((in_ref, pr_ref, ct_ref))
     ]
     for cp in raw_copies:
@@ -120,6 +120,13 @@
             x_copy(j, a).wait_recv()
             y_copy(j, a, g).start()
 
+    def forward_next(q):
+        for a in range(3):
+            @pl.when((q % 3 == a) & (q < 3 * pieces))
+            def _():
+                x_copy(q // 3, a).wait_recv()
+                y_copy(q // 3, a, g).start()
+
     def y_arrived(j):
         for a in range(3):
             y_copy(j, a, 1 - g).wait_recv()
@@ -179,7 +186,6 @@
         x_start(j)
     for a in range(3):
         raw_copies[a].wait()
-        xt[a, rows_of(c, d), :] = raw[a].T
     z_start(0, True)
     z_start(0, False)
     sib_copy(c).start()
@@ -187,6 +193,22 @@
         cp.start()
     acc[...] = jnp.zeros_like(acc)
 
+    blocks = half // 128
+
+    def token_major(h):
+        for src in range(n // 2):
+            sib_copy(h * (n // 2) + src, dd=1 - d).wait_recv()
+
+        @pl.loop(0, blocks)
+        def _(j):
+            feat = pl.ds(pl.multiple_of(h * half + j * 128, 128), 128)
+            lane = pl.ds(pl.multiple_of(j * 128, 128), 128)
+            xs[h, :tokens, lane] = xt[0, feat, :].T
+            xs[h, tokens:, lane] = xt[1, feat, :].T
+            cot[h, :, lane] = xt[2, feat, :].T
+
+    side = (2 * c) // n
+    near = n // 2 - 1
     lead = 2 * (n - 1)
     for j in range(lead):
         forward(j)
@@ -195,32 +217,34 @@
         if j % 2:
             z_got(j // 2, True)
             z_got(j // 2, False)
-
+        if j == 2 * near:
+            token_major(side)
     for cp in own_copies:
         cp.wait()
-    for src in range(n):
-        sib_copy(src, dd=1 - d).wait_recv()
-
-    blocks = half // 128
-    for h in range(2):
-        @pl.loop(0, blocks)
-        def _(j):
-            feat = pl.ds(pl.multiple_of(h * half + j * 128, 128), 128)
-            lane = pl.ds(pl.multiple_of(j * 128, 128), 128)
-            xs[h, :tokens, lane] = xt[0, feat, :].T
-            xs[h, tokens:, lane] = xt[1, feat, :].T
-            cot[h, :, lane] = xt[2, feat, :].T
-
-    def compute(off, width):
+    token_major(1 - side)
+
+    def forward_half(off, width, last=None):
         col = pl.ds(off, width)
-        gates = nn(xs[r], own_g[:, col]) + nn(xs[1 - r], far_g[:, col])
-        ups = nn(xs[r], own_u[:, col]) + nn(xs[1 - r], far_u[:, col])
-        back = nt(cot[r], own_d[col, :]) + nt(cot[1 - r], far_d[col, :])
+        gates, ups = nn(xs[r], own_g[:, col]), nn(xs[r], own_u[:, col])
+        back = nt(cot[r], own_d[col, :])
+        if last is not None:
+            y_copy(last, 0, 1 - g).wait_recv()
+        gates = gates + nn(xs[1 - r], far_g[:, col])
+        if last is not None:
+            y_copy(last, 1, 1 - g).wait_recv()
+        ups = ups + nn(xs[1 - r], far_u[:, col])
+        if last is not None:
+            y_copy(last, 2, 1 - g).wait_recv()
+        back = back + nt(cot[1 - r], far_d[col, :])
         pre_gate, tan_gate = gates[:tokens], gates[tokens:]
         pre_up, tan_up = ups[:tokens], ups[tokens:]
         slope, bend = slope_and_bend(pre_gate)
         gate_part = (back * (tan_up * slope + pre_up * bend * tan_gate)).astype(BF16)
         up_part = (back * slope * tan_gate).astype(BF16)
+        return gate_part, up_part
+
+    def backward_half(off, width, gate_part, up_part):
+        col = pl.ds(off, width)
         for w_g, w_u, base in ((own_g, own_u, r), (far_g, far_u, 1 - r)):
             for q in range(0, half, part):
                 rows = pl.ds(pl.multiple_of(base * half + q, 32), part)
@@ -231,22 +255,25 @@
     per = WIDE // PIECE
     steps = hidden // WIDE
 
+    begin = 3 * lead + 2
+    forward_next(begin - 2)
+    forward_next(begin - 1)
+
     @pl.loop(0, steps)
     def _(i):
         for k in range(per):
             y_arrived(i * per + k)
-
-        compute(pl.multiple_of(i * WIDE, WIDE), WIDE)
-
-        @pl.when(lead + i < pieces)
-        def _():
-            forward(lead + i)
-
-    for j in range(lead + steps, pieces):
-        forward(j)
+        off = pl.multiple_of(i * WIDE, WIDE)
+        parts = forward_half(off, WIDE)
+        forward_next(begin + 2 * i)
+        backward_half(off, WIDE, *parts)
+        forward_next(begin + 2 * i + 1)
+
+    for q in range(begin + 2 * steps, 3 * pieces):
+        forward_next(q)
     for j in range(steps * per, pieces):
-        y_arrived(j)
-        compute(j * PIECE, PIECE)
+        off = j * PIECE
+        backward_half(off, PIECE, *forward_half(off, PIECE, j))
 
     def q_copy(cc):
         return pltpu.make_async_remote_copy(
@@ -254,8 +281,6 @@
             send_sem=qsend.at[cc], recv_sem=qrecv.at[cc],
             device_id=sib, device_id_type=MESH,
         )
-
-    side = (2 * c) // n
 
     def q_order(i):
         return (n - 1 - i) * (1 - side) + i * side
@@ -341,7 +366,6 @@
         in_specs=[any_spec] * 6,
         out_specs=pl.BlockSpec(memory_space=pltpu.VMEM),
         scratch_shapes=[
-            vmem((3, tokens, part), BF16),
             vmem((3, wide, tokens), BF16),
             vmem((2, 2 * tokens, half), BF16),
             vmem((2, tokens, half), BF16),
@@ -364,7 +388,7 @@
             bytes_accessed=6 * half * hidden,
             transcendentals=tokens * hidden,
         ),
-    )(inputs, probe, cotangent, gate_weight, up_weight, down_weight)
+    )(inputs.T, probe.T, cotangent.T, gate_weight, up_weight, down_weight)
     return out.T
 
 

time: 143 us -> 133 us (0.930)
  local copies, waits for them, and re-layouts: 7.32 us -> 1.69 us
  Pallas kernels: 135 us -> 131 us
    unnamed x4 -> x1, local copies, waits for them, and re-layouts: 7.32 us -> 1.69 us
    pallas_call x1, Pallas kernels: 135 us -> 131 us  [fused(): pl.pallas_call(functools.partial(kernel, n), out_shape=jax.ShapeDtypeStru...]
where the time goes in v3:
time: 133 us
  Pallas kernels  131 us (98%)
  local copies, waits for them, and re-layouts  1.69 us (1%)
    pallas_call x1, Pallas kernels, fused(): pl.pallas_call(functools.partial(kernel, n), out_shape=jax.ShapeDtypeStru...  131 us

profile of v3, /device:TPU:0, one launch (start us, length us, event | category | flops | bytes accessed | tf_op | source)
XLA Modules:
  0.0 132.6 jit_solution(14150052906958313894)
XLA Ops:
  0.0 130.9 %shard_map.64 = bf16[288,512]{1,0:T(8,128)(2,1)} custom-call(bf16[288,512]{1,0:T(8,128)(2,1)} %bitcast.5, bf16[288,512]{1,0:T(8,128)(2,1)} %bitcast.6, bf16[288,512]{1,0:T(8,128)(2,1)} %bitcast.7, bf16[1152,1152]{1,0:T(8,128)(2,1)} %gw_ref.1, bf16[1152,1152]{1,0:T(8,128)(2,1)} %uw_ref.1, bf16[1152,1152]{1,0:T(8,128)(2,1)} %dw_ref.1), custom_call_target="tpu_custom_call" | custom-call | flops 19025362944 | bytes 7962624 | tf_op jit(solution)/shard_map/pallas_call | solution.py:363
  130.9 1.7 %copy.8 = bf16[512,288]{0,1:T(8,128)(2,1)} copy(bf16[512,288]{0,1:T(8,128)(2,1)} %bitcast.4) | data formatting | bytes 589824

commit v4 on v3

--- a/solution.py
+++ b/solution.py
@@ -90,21 +90,24 @@
     def windows(j, w):
         col = pl.ds(pl.multiple_of(j * PIECE, PIECE), PIECE)
         row = pl.ds(pl.multiple_of(w * hd, 32), hd)
-        hrow = pl.ds(pl.multiple_of(j * PIECE + w * (PIECE // 2), 64), PIECE // 2)
-        return (row, col), (row, col), (hrow, slice(None))
+        quarter = PIECE // 4
+        first = pl.multiple_of(j * PIECE + w * (PIECE // 2), 64)
+        second = pl.multiple_of(j * PIECE + w * (PIECE // 2) + quarter, 32)
+        low, high = pl.ds(first, quarter), pl.ds(second, quarter)
+        return (row, col), (row, col), (low, slice(None)), (high, slice(None))
 
     def x_copy(j, a):
         win = windows(j, g)[a]
         return pltpu.make_async_remote_copy(
-            src_ref=(gw_ref, uw_ref, dw_ref)[a].at[win],
-            dst_ref=(far_g, far_u, far_d)[a].at[win],
+            src_ref=(gw_ref, uw_ref, dw_ref, dw_ref)[a].at[win],
+            dst_ref=(far_g, far_u, far_d, far_d)[a].at[win],
             send_sem=xsend.at[j, a], recv_sem=xrecv.at[j, a],
             device_id=x_dev, device_id_type=MESH,
         )
 
     def y_copy(j, a, w):
         win = windows(j, w)[a]
-        far = (far_g, far_u, far_d)[a].at[win]
+        far = (far_g, far_u, far_d, far_d)[a].at[win]
         return pltpu.make_async_remote_copy(
             src_ref=far, dst_ref=far,
             send_sem=ysend.at[j, a], recv_sem=yrecv.at[j, a],
@@ -112,23 +115,23 @@
         )
 
     def x_start(j):
-        for a in range(3):
+        for a in range(4):
             x_copy(j, a).start()
 
     def forward(j):
-        for a in range(3):
+        for a in range(4):
             x_copy(j, a).wait_recv()
             y_copy(j, a, g).start()
 
     def forward_next(q):
-        for a in range(3):
-            @pl.when((q % 3 == a) & (q < 3 * pieces))
+        for a in range(4):
+            @pl.when((q % 4 == a) & (q < 4 * pieces))
             def _():
-                x_copy(q // 3, a).wait_recv()
-                y_copy(q // 3, a, g).start()
+                x_copy(q // 4, a).wait_recv()
+                y_copy(q // 4, a, g).start()
 
     def y_arrived(j):
-        for a in range(3):
+        for a in range(4):
             y_copy(j, a, 1 - g).wait_recv()
 
     def z_copy(s, right):
@@ -235,6 +238,7 @@
         ups = ups + nn(xs[1 - r], far_u[:, col])
         if last is not None:
             y_copy(last, 2, 1 - g).wait_recv()
+            y_copy(last, 3, 1 - g).wait_recv()
         back = back + nt(cot[1 - r], far_d[col, :])
         pre_gate, tan_gate = gates[:tokens], gates[tokens:]
         pre_up, tan_up = ups[:tokens], ups[tokens:]
@@ -255,8 +259,7 @@
     per = WIDE // PIECE
     steps = hidden // WIDE
 
-    begin = 3 * lead + 2
-    forward_next(begin - 2)
+    begin = 4 * lead + 1
     forward_next(begin - 1)
 
     @pl.loop(0, steps)
@@ -265,11 +268,12 @@
             y_arrived(i * per + k)
         off = pl.multiple_of(i * WIDE, WIDE)
         parts = forward_half(off, WIDE)
-        forward_next(begin + 2 * i)
+        forward_next(begin + 3 * i)
+        forward_next(begin + 3 * i + 1)
         backward_half(off, WIDE, *parts)
-        forward_next(begin + 2 * i + 1)
-
-    for q in range(begin + 2 * steps, 3 * pieces):
+        forward_next(begin + 3 * i + 2)
+
+    for q in range(begin + 3 * steps, 4 * pieces):
         forward_next(q)
     for j in range(steps * per, pieces):
         off = j * PIECE
@@ -290,50 +294,54 @@
         sib_out[t] = acc[rows_of(t, 1 - d), :].astype(BF16)
         q_copy(t).start()
 
-    def z_sum(way, t):
-        return pltpu.make_async_remote_copy(
-            src_ref=z_out.at[t], dst_ref=z_in.at[way, t],
-            send_sem=zsend.at[t], recv_sem=zrecv.at[way, t],
-            device_id=at(cc=c + 1 - 2 * way), device_id_type=MESH,
-        )
-
-    def z_came(way, t):
-        return pltpu.make_async_remote_copy(
-            src_ref=z_out.at[t], dst_ref=z_in.at[way, t],
-            send_sem=zsend.at[t], recv_sem=zrecv.at[way, t],
-            device_id=at(cc=c - 1 + 2 * way), device_id_type=MESH,
-        )
-
-    def fed(way):
-        return c * (1 - way) + (n - 1 - c) * way > 0
-
-    def add_in(way, t):
-        @pl.when(fed(way))
+    cut = part // 2
+
+    def z_sum(way, t, h, back=False):
+        rows = pl.ds(h * cut, cut)
+        step = 1 - 2 * way
+        return pltpu.make_async_remote_copy(
+            src_ref=z_out.at[t, rows], dst_ref=z_in.at[way, t, rows],
+            send_sem=zsend.at[t, h], recv_sem=zrecv.at[way, t, h],
+            device_id=at(cc=c - step if back else c + step), device_id_type=MESH,
+        )
+
+    def shard(t, h):
+        return pl.ds(pl.multiple_of((t * 2 + d) * part + h * cut, 16), cut)
+
+    def add_in(way, t, h):
+        @pl.when(c * (1 - way) + (n - 1 - c) * way > 0)
         def _():
-            z_came(way, t).wait_recv()
-            rows = rows_of(t, d)
-            acc[rows, :] += z_in[way, t].astype(F32)
+            z_sum(way, t, h, back=True).wait_recv()
+            acc[shard(t, h), :] += z_in[way, t, h * cut:(h + 1) * cut].astype(F32)
+
+    def with_pair(t, h):
+        other = sib_in[t, h * cut:(h + 1) * cut].astype(F32)
+        return (acc[shard(t, h), :] + other).astype(BF16)
 
     def pass_on(way, t):
         @pl.when((t - c) * (1 - 2 * way) > 0)
         def _():
-            add_in(way, t)
-            z_out[t] = (acc[rows_of(t, d), :] + sib_in[t].astype(F32)).astype(BF16)
-            z_sum(way, t).start()
-
-    for i in range(n):
-        t = q_order(i)
-        q_copy(t).wait_recv()
-        pass_on(side, t)
+            for h in range(2):
+                add_in(way, t, h)
+                z_out[t, h * cut:(h + 1) * cut] = with_pair(t, h)
+                z_sum(way, t, h).start()
+
     for i in range(n - 1):
-        pass_on(1 - side, n - 1 - q_order(i))
-    add_in(side, c)
-    add_in(1 - side, c)
-    out_ref[...] = (acc[rows_of(c, d), :] + sib_in[c].astype(F32)).astype(BF16)
+        if i == 0:
+            q_copy(q_order(0)).wait_recv()
+        pass_on(side, q_order(i))
+        if i == 0:
+            for k in range(1, n):
+                q_copy(q_order(k)).wait_recv()
+        pass_on(1 - side, q_order(n - 1 - i))
+    for h in range(2):
+        add_in(side, c, h)
+        add_in(1 - side, c, h)
+        out_ref[h * cut:(h + 1) * cut, :] = with_pair(c, h)
 
     @pl.loop(0, pieces)
     def _(j):
-        for a in range(3):
+        for a in range(4):
             x_copy(j, a).wait_send()
             y_copy(j, a, g).wait_send()
 
@@ -349,7 +357,8 @@
         for way, away in ((0, t > c), (1, t < c)):
             @pl.when(away)
             def _():
-                z_sum(way, t).wait_send()
+                for h in range(2):
+                    z_sum(way, t, h).wait_send()
 
 
 def fused(n, inputs, probe, cotangent, gate_weight, up_weight, down_weight):
@@ -375,10 +384,10 @@
             vmem((n, part, tokens), BF16), vmem((n, part, tokens), BF16),
             vmem((n, part, tokens), BF16), vmem((2, n, part, tokens), BF16),
             dma((6,)),
-            dma((pieces, 3)), dma((pieces, 3)), dma((pieces, 3)), dma((pieces, 3)),
+            dma((pieces, 4)), dma((pieces, 4)), dma((pieces, 4)), dma((pieces, 4)),
             dma((n - 1,)), dma((n - 1,)), dma((n - 1,)), dma((n - 1,)),
             dma((n,)), dma((n,)), dma((n,)), dma((n,)),
-            dma((n,)), dma((2, n)),
+            dma((n, 2)), dma((2, n, 2)),
         ],
         compiler_params=pltpu.CompilerParams(
             collective_id=0, has_side_effects=True, vmem_limit_bytes=60 * 2**20

time: 133 us -> 129 us (0.970)
  Pallas kernels: 131 us -> 127 us
    pallas_call x1, Pallas kernels: 131 us -> 127 us  [fused(): pl.pallas_call(functools.partial(kernel, n), out_shape=jax.ShapeDtypeStru...]
where the time goes in v4:
time: 129 us; the launch traced here: 128 us
  Pallas kernels  127 us (98%)
  local copies, waits for them, and re-layouts  1.69 us (1%)
    pallas_call x1, Pallas kernels, fused(): pl.pallas_call(functools.partial(kernel, n), out_shape=jax.ShapeDtypeStru...  127 us

profile of v4, /device:TPU:0, one launch (start us, length us, event | category | flops | bytes accessed | tf_op | source)
XLA Modules:
  0.0 128.4 jit_solution(13190346993150007046)
XLA Ops:
  0.0 126.6 %shard_map.64 = bf16[288,512]{1,0:T(8,128)(2,1)} custom-call(bf16[288,512]{1,0:T(8,128)(2,1)} %bitcast.5, bf16[288,512]{1,0:T(8,128)(2,1)} %bitcast.6, bf16[288,512]{1,0:T(8,128)(2,1)} %bitcast.7, bf16[1152,1152]{1,0:T(8,128)(2,1)} %gw_ref.1, bf16[1152,1152]{1,0:T(8,128)(2,1)} %uw_ref.1, bf16[1152,1152]{1,0:T(8,128)(2,1)} %dw_ref.1), custom_call_target="tpu_custom_call" | custom-call | flops 19025362944 | bytes 7962624 | tf_op jit(solution)/shard_map/pallas_call | solution.py:372
  126.7 1.7 %copy.8 = bf16[512,288]{0,1:T(8,128)(2,1)} copy(bf16[512,288]{0,1:T(8,128)(2,1)} %bitcast.4) | data formatting | bytes 589824

commit v5 on v4

--- a/solution.py
+++ b/solution.py
@@ -247,9 +247,10 @@
         up_part = (back * slope * tan_gate).astype(BF16)
         return gate_part, up_part
 
-    def backward_half(off, width, gate_part, up_part):
+    def backward_half(off, width, gate_part, up_part, which=(0, 1)):
         col = pl.ds(off, width)
-        for w_g, w_u, base in ((own_g, own_u, r), (far_g, far_u, 1 - r)):
+        for k in which:
+            w_g, w_u, base = ((own_g, own_u, r), (far_g, far_u, 1 - r))[k]
             for q in range(0, half, part):
                 rows = pl.ds(pl.multiple_of(base * half + q, 32), part)
                 acc[rows, :] += nt(w_g[q:q + part, col], gate_part) + nt(
@@ -275,10 +276,6 @@
 
     for q in range(begin + 3 * steps, 4 * pieces):
         forward_next(q)
-    for j in range(steps * per, pieces):
-        off = j * PIECE
-        backward_half(off, PIECE, *forward_half(off, PIECE, j))
-
     def q_copy(cc):
         return pltpu.make_async_remote_copy(
             src_ref=sib_out.at[cc], dst_ref=sib_in.at[cc],
@@ -289,10 +286,25 @@
     def q_order(i):
         return (n - 1 - i) * (1 - side) + i * side
 
-    for i in range(n):
+    def pair_send(i):
         t = q_order(i)
         sib_out[t] = acc[rows_of(t, 1 - d), :].astype(BF16)
         q_copy(t).start()
+
+    tail = range(steps * per, pieces)
+    for j in tail:
+        off = j * PIECE
+        parts = forward_half(off, PIECE, j)
+        for k in range(2):
+            @pl.when((r + 1 - side) % 2 == k)
+            def _():
+                backward_half(off, PIECE, *parts, which=(k,))
+                if j == pieces - 1:
+                    for i in range(n // 2):
+                        pair_send(i)
+                backward_half(off, PIECE, *parts, which=(1 - k,))
+    for i in range(n // 2 if len(tail) else 0, n):
+        pair_send(i)
 
     cut = part // 2
 

time: 129 us -> 130 us (level)
  no operation moved by 1% of the time
where the time goes in v5:
time: 130 us; the launch traced here: 129 us
  Pallas kernels  128 us (98%)
  local copies, waits for them, and re-layouts  1.69 us (1%)
    pallas_call x1, Pallas kernels, fused(): pl.pallas_call(functools.partial(kernel, n), out_shape=jax.ShapeDtypeStru...  128 us

profile of v5, /device:TPU:0, one launch (start us, length us, event | category | flops | bytes accessed | tf_op | source)
XLA Modules:
  0.0 129.2 jit_solution(453061155292623072)
XLA Ops:
  0.0 127.5 %shard_map.64 = bf16[288,512]{1,0:T(8,128)(2,1)} custom-call(bf16[288,512]{1,0:T(8,128)(2,1)} %bitcast.5, bf16[288,512]{1,0:T(8,128)(2,1)} %bitcast.6, bf16[288,512]{1,0:T(8,128)(2,1)} %bitcast.7, bf16[1152,1152]{1,0:T(8,128)(2,1)} %gw_ref.1, bf16[1152,1152]{1,0:T(8,128)(2,1)} %uw_ref.1, bf16[1152,1152]{1,0:T(8,128)(2,1)} %dw_ref.1), custom_call_target="tpu_custom_call" | custom-call | flops 19025362944 | bytes 7962624 | tf_op jit(solution)/shard_map/pallas_call | solution.py:384
  127.5 1.7 %copy.8 = bf16[512,288]{0,1:T(8,128)(2,1)} copy(bf16[512,288]{0,1:T(8,128)(2,1)} %bitcast.4) | data formatting | bytes 589824
